TPU v7x, 512 devices: a whole 4x8x8 slice. The times are simulated.
512 devices in a mesh: seq: 64 (over z, y), head: 8 (over x, core).
Axes of the slice: x: 4, y: 8, z: 8, core: 2. Of those that a mesh axis runs over, the one named last changes fastest.
Arguments:
- query: bfloat16 [16384, 3072], P('seq', 'head'), may hold values from -120 to 120
- keys: bfloat16 [16384, 3072], P('seq', 'head'), may hold values from -4.1 to 4.1
- values: bfloat16 [16384, 3072], P('seq', 'head'), may hold values from -6 to 6
- shot_ids: int32 [16384], replicated, may hold values from 0 to 31, never falling along the last dimension, each value on 1 to 1025 neighbouring positions
- routes: int32 [256, 8], replicated, may hold values from 0 to 255, as said below
- out_weight: bfloat16 [3072, 3072], P('head'), may hold values from -0.15625 to 0.15625
Outputs:
- mixed_out: bfloat16 [16384, 3072], P('seq', 'head')
Inputs may be any that keep to these rules, and one draw needn't show every extreme that they name: `shot_ids`: shots are runs of equal numbers that never fall, each of 1 to 1025 tokens, one exactly 1025. The 8 routes of a query stretch name different stretches. Over the query stretches of one seq index (aligned blocks of 4 rows), the routes name at most 1 stretches of any one seq index's block of 4 stretches, all different, and exactly 1 for some block in every draw.
All inputs are finite; a program needn't handle non-finite values.
Results may differ from a plain program's by a relative error of at most 0.017.
Values may be sent and summed in bfloat16 or wider, within the bound.
A program may use at most 128 MiB of HBM per device.

v0:
```python
import jax
import jax.numpy as jnp
from jax import lax
from jax.sharding import PartitionSpec as P

HEAD_DIM = 128
STRETCH = 64
REACH = 4


NEGATIVE = -1e30


def from_behind(value, axis, steps):
    count = lax.axis_size(axis)
    first, last = (max(0, -steps), min(count, count - steps))
    return lax.ppermute(value, axis, [(source, source + steps) for source in range(first, last)])


def rounded(array):
    return lax.optimization_barrier(array.astype(jnp.bfloat16)).astype(jnp.float32)


def rank_tables(routes, position, devices, stretch_count, capacity):
    total = stretch_count * routes.shape[1]
    route_all = routes.reshape(devices, total)
    owner_all = route_all // stretch_count
    order = jnp.arange(total, dtype=jnp.int32)
    earlier = order[:, None] > order[None, :]
    same_owner = owner_all[:, :, None] == owner_all[:, None, :]
    rank_all = jnp.sum(jnp.where(same_owner & earlier[None], 1, 0), axis=2).astype(jnp.int32)
    slot_ids = jnp.arange(capacity, dtype=jnp.int32)
    served = (owner_all == position)[:, :, None] & (rank_all[:, :, None] == slot_ids[None, None, :])
    local_pick = jnp.sum(jnp.where(served, (route_all % stretch_count)[:, :, None], 0), axis=1)
    my_owner = lax.dynamic_index_in_dim(owner_all, position, 0, keepdims=False)
    my_rank = lax.dynamic_index_in_dim(rank_all, position, 0, keepdims=False)
    return (local_pick, my_owner, my_rank, slot_ids)


def neighbour(stacked, distance):
    return from_behind(stacked, "seq", distance)


def shards(query, keys, values, shot_ids, routes, out_weight):
    local_rows, width = query.shape
    heads = width // HEAD_DIM
    scale = HEAD_DIM ** (-0.5)
    devices = lax.axis_size("seq")
    position = lax.axis_index("seq")
    stretch_count = local_rows // STRETCH
    routes_each = routes.shape[1]
    total = stretch_count * routes_each
    capacity = max(1, (total + devices - 1) // devices)
    block_rows = min(512, local_rows)
    blocks = local_rows // block_rows
    per_block = block_rows // STRETCH
    span_rows = (2 * REACH + 1) * local_rows
    local_pick, my_owner, my_rank, slot_ids = rank_tables(
        routes, position, devices, stretch_count, capacity
    )
    my_slot = my_owner * capacity + my_rank
    filler = jnp.full((REACH * local_rows,), -1, jnp.int32)
    window_ids = lax.dynamic_slice_in_dim(
        jnp.concatenate([filler, shot_ids, filler]), position * local_rows, span_rows
    )
    own_ids = lax.dynamic_slice_in_dim(shot_ids, position * local_rows, local_rows)
    stacked = jnp.stack([keys, values])
    lower_parts = [neighbour(stacked, distance) for distance in range(REACH, 0, -1)]
    upper_parts = [neighbour(stacked, -distance) for distance in range(1, REACH + 1)]
    window = jnp.concatenate(lower_parts + [stacked] + upper_parts, axis=1)
    stretched = stacked.reshape(2, stretch_count, STRETCH, width)

    def shot_part(head, block):
        query_block = lax.dynamic_slice(
            query, (block * block_rows, head * HEAD_DIM), (block_rows, HEAD_DIM)
        )
        window_keys = lax.dynamic_slice(window[0], (0, head * HEAD_DIM), (span_rows, HEAD_DIM))
        window_values = lax.dynamic_slice(window[1], (0, head * HEAD_DIM), (span_rows, HEAD_DIM))
        scores = (
            jnp.einsum("qd,kd->qk", query_block, window_keys, preferred_element_type=jnp.float32)
            * scale
        )
        scores = jnp.where(own_ids[:, None] == window_ids[None, :], scores, NEGATIVE)
        top = jnp.max(scores, axis=1)
        weights = jnp.exp(scores - top[:, None])
        mass = jnp.sum(weights, axis=1)
        summed = jnp.dot(
            weights.astype(jnp.bfloat16), window_values, preferred_element_type=jnp.float32
        )
        return (
            query_block,
            top.reshape(per_block, STRETCH),
            mass.reshape(per_block, STRETCH),
            summed.reshape(per_block, STRETCH, HEAD_DIM),
        )

    incoming = lax.all_to_all(
        stretched[:, local_pick], "seq", split_axis=1, concat_axis=1, tiled=True
    )
    routed = incoming.reshape(2, devices * capacity, STRETCH, width)[:, my_slot]
    routed = routed.reshape(2, stretch_count, routes_each, STRETCH, width)

    def routed_part(head, block, query_block):
        corner = (block * per_block, 0, 0, head * HEAD_DIM)
        extent = (per_block, routes_each, STRETCH, HEAD_DIM)
        routed_keys = lax.dynamic_slice(routed[0], corner, extent)
        routed_values = lax.dynamic_slice(routed[1], corner, extent)
        grouped = query_block.reshape(per_block, STRETCH, HEAD_DIM)
        scores = (
            jnp.einsum("cqd,cjkd->cqjk", grouped, routed_keys, preferred_element_type=jnp.float32)
            * scale
        )
        top = jnp.max(scores, axis=3)
        weights = jnp.exp(scores - top[..., None])
        mass = jnp.sum(weights, axis=3)
        summed = jnp.einsum(
            "cqjk,cjkd->cqjd",
            weights.astype(jnp.bfloat16),
            routed_values,
            preferred_element_type=jnp.float32,
        )
        return (top, mass, rounded(summed / mass[..., None]))

    def single(index):
        head = index // blocks
        block = index % blocks
        query_block, shot_top, shot_mass, shot_sum = shot_part(head, block)
        routed_top, routed_mass, routed_mean = routed_part(head, block, query_block)
        overall = jnp.maximum(shot_top, jnp.max(routed_top, axis=2))
        shot_factor = jnp.exp(shot_top - overall)
        routed_factor = jnp.exp(routed_top - overall[..., None])
        denominator = shot_factor * shot_mass + jnp.sum(routed_factor * routed_mass, axis=2)
        summed = shot_factor[..., None] * shot_sum + jnp.sum(
            (routed_factor * routed_mass)[..., None] * routed_mean, axis=2
        )
        return (summed / denominator[..., None]).reshape(block_rows, HEAD_DIM)

    pieces = lax.map(single, jnp.arange(heads * blocks, dtype=jnp.int32))
    attended = jnp.transpose(pieces, (1, 0, 2)).reshape(local_rows, width).astype(jnp.bfloat16)
    partial_value = jnp.dot(attended, out_weight, preferred_element_type=jnp.float32)
    mixed = lax.psum_scatter(
        partial_value.astype(jnp.bfloat16), "head", scatter_dimension=1, tiled=True
    )
    return mixed


def solution(mesh):
    placed = (P("seq", "head"), P("seq", "head"), P("seq", "head"), P(), P(), P("head", None))
    return jax.shard_map(
        shards, mesh=mesh, in_specs=placed, out_specs=P("seq", "head"), check_vma=False
    )
```

profile of v0, /device:TPU:8, one launch (start us, length us, event | category | flops | bytes accessed | tf_op | source)
XLA Modules:
  0.0 467.8 jit_solution(5367751177942376741)
XLA Ops:
  6.5 1.0 copy.51
  8.7 1.1 pad_maximum_fusion.1
  9.8 4.1 gather_fusion
  13.8 16.9 %all-to-all-start = ((bf16[2,64,1,64,384]{4,3,0,2,1:T(8,128)(2,1)}), bf16[2,64,1,64,384]{4,3,0,2,1:T(8,128)(2,1)}, u32[]{:S(2)}, u32[]{:S(2)}) async-start(bf16[2,64,1,64,384]{4,3,0,2,1:T(8,128)(2,1)} %bitcast.86), calls=%async_computation | async-start | bytes 12582912 | tf_op jit(solution)/shard_map/all_to_all | solution.py:97
  30.9 7.2 %collective-permute-start = (bf16[2,256,384]{2,1,0:T(8,128)(2,1)S(1)}, bf16[2,256,384]{2,1,0:T(8,128)(2,1)}, u32[]{:S(2)}, u32[]{:S(2)}) collective-permute-start(bf16[2,256,384]{2,1,0:T(8,128)(2,1)S(1)} %pad_maximum_fusion), channel_id=1, source_target_pairs={{0,32},{8,40},{16,48},{24,56},{32,64},{40,72},{48,80},{56,88},{64,... | collective-permute-start | bytes 1179656 | tf_op jit(solution)/shard_map/ppermute | solution.py:17
  38.0 3.4 collective-permute-start.1
  41.4 4.3 collective-permute-start.2
  45.7 2.6 collective-permute-start.3
  48.3 4.0 collective-permute-start.4
  52.3 0.9 add_reduce_fusion
  53.7 0.8 fusion.30
  54.5 0.7 pad_clamp_fusion
  55.1 1.3 dynamic_slice.49
  56.5 125.6 %collective-permute-done = bf16[2,256,384]{2,1,0:T(8,128)(2,1)} collective-permute-done((bf16[2,256,384]{2,1,0:T(8,128)(2,1)S(1)}, bf16[2,256,384]{2,1,0:T(8,128)(2,1)}, u32[]{:S(2)}, u32[]{:S(2)}) %collective-permute-start) | collective-permute-done | bytes 393248 | tf_op jit(solution)/shard_map/ppermute | solution.py:17
  182.0 1.3 collective-permute-start.5
  183.3 1.8 constant_dynamic-update-slice_fusion.9
  185.1 43.2 %collective-permute-done.1 = bf16[2,256,384]{2,1,0:T(8,128)(2,1)} collective-permute-done((bf16[2,256,384]{2,1,0:T(8,128)(2,1)S(1)}, bf16[2,256,384]{2,1,0:T(8,128)(2,1)}, u32[]{:S(2)}, u32[]{:S(2)}) %collective-permute-start.1) | collective-permute-done | bytes 393248 | tf_op jit(solution)/shard_map/ppermute | solution.py:17
  228.3 1.3 collective-permute-start.6
  229.6 1.8 constant_dynamic-update-slice_fusion.8
  231.4 36.1 %collective-permute-done.2 = bf16[2,256,384]{2,1,0:T(8,128)(2,1)} collective-permute-done((bf16[2,256,384]{2,1,0:T(8,128)(2,1)S(1)}, bf16[2,256,384]{2,1,0:T(8,128)(2,1)}, u32[]{:S(2)}, u32[]{:S(2)}) %collective-permute-start.2) | collective-permute-done | bytes 393248 | tf_op jit(solution)/shard_map/ppermute | solution.py:17
  267.5 1.3 collective-permute-start.7
  268.8 1.8 constant_dynamic-update-slice_fusion.7
  270.6 5.3 %collective-permute-done.3 = bf16[2,256,384]{2,1,0:T(8,128)(2,1)} collective-permute-done((bf16[2,256,384]{2,1,0:T(8,128)(2,1)S(1)}, bf16[2,256,384]{2,1,0:T(8,128)(2,1)}, u32[]{:S(2)}, u32[]{:S(2)}) %collective-permute-start.3) | collective-permute-done | bytes 393248 | tf_op jit(solution)/shard_map/ppermute | solution.py:17
  275.9 1.8 constant_dynamic-update-slice_fusion.6
  277.7 0.8 constant_dynamic-update-slice_fusion.5
  278.4 0.8 constant_dynamic-update-slice_fusion.4
  279.3 0.8 constant_dynamic-update-slice_fusion.3
  280.1 0.8 constant_dynamic-update-slice_fusion.2
  280.9 27.7 %collective-permute-done.7 = bf16[2,256,384]{2,1,0:T(8,128)(2,1)S(1)} collective-permute-done((bf16[2,256,384]{2,1,0:T(8,128)(2,1)S(1)}, bf16[2,256,384]{2,1,0:T(8,128)(2,1)S(1)}, u32[]{:S(2)}, u32[]{:S(2)}) %collective-permute-start.7) | collective-permute-done | bytes 393248 | tf_op jit(solution)/shard_map/ppermute | solution.py:17
  308.5 0.8 constant_dynamic-update-slice_fusion.1
  309.3 6.3 %copy.72 = bf16[2,64,1,64,384]{4,3,1,0,2:T(8,128)(2,1)} copy(bf16[2,64,1,64,384]{4,3,0,2,1:T(8,128)(2,1)} %all-to-all-done) | data formatting | bytes 12582912 | tf_op jit(solution)/shard_map/all_to_all | solution.py:97
  315.6 5.5 %gather_fusion.1 = bf16[32,2,64,384]{3,2,1,0:T(8,128)(2,1)} fusion(bf16[2,64,64,384]{3,2,1,0:T(8,128)(2,1)} %bitcast.87, s32[1024]{0:T(1024)S(1)} %pad_clamp_fusion), kind=kCustom, calls=%fused_computation.1 | custom fusion | bytes 6291584 | tf_op jit(solution)/shard_map/gather | solution.py:100
  321.1 4.0 copy.63
  325.1 60.9 %while.12 = (s32[]{:T(128)}, bf16[3,256,128]{1,2,0:T(8,128)(2,1)}, s32[256]{0:T(256)S(1)}, s32[2304]{0:T(1024)S(1)}, s32[3]{0:T(128)S(1)}, /*index=5*/bf16[256,3...) while((s32[]{:T(128)}, bf16[3,256,128]{1,2,0:T(8,128)(2,1)}, ...), condition=%wide.region_11.12_spmd, body=%wide.region_3.11_spmd.sunk | while | flops 375556096 | bytes 30977756 | solution.py:138
  325.1 0.6 dynamic_slice.106
  326.3 0.8 constant_dynamic-slice_fusion.3
  327.1 3.5 fusion.62
  331.2 3.6 fusion.66
  334.8 2.8 fusion.67
  337.7 3.2 fusion.69
  341.0 1.7 fusion.65
  343.1 1.5 fusion.70
  344.7 0.6 constant_dynamic-update-slice_fusion.11
  345.4 0.6 dynamic_slice.106
  346.6 0.8 constant_dynamic-slice_fusion.3
  347.4 3.5 fusion.62
  351.5 3.6 fusion.66
  355.1 2.8 fusion.67
  358.1 3.2 fusion.69
  361.3 1.7 fusion.65
  363.4 1.5 fusion.70
  365.0 0.6 constant_dynamic-update-slice_fusion.11
  366.9 0.8 constant_dynamic-slice_fusion.3
  367.8 3.5 fusion.62
  371.8 3.6 fusion.66
  375.4 2.8 fusion.67
  378.4 3.2 fusion.69
  381.6 1.7 fusion.65
  383.7 1.5 fusion.70
  385.4 0.6 constant_dynamic-update-slice_fusion.11
  386.0 3.1 convolution_convert_fusion
  389.1 2.6 copy.67
  391.7 67.5 %reduce-scatter.4.cloned.1.call-done = bf16[384,256]{1,0:T(8,128)(2,1)} async-done(((bf16[3072,256]{1,0:T(8,128)(2,1)}), bf16[384,256]{1,0:T(8,128)(2,1)}) %reduce-scatter.4.cloned.1.call-update) | async-done | bytes 196624
  459.2 1.7 copy.68
  (68 shorter events, 6.0 us)
Async XLA Ops:
  6.5 379.5 %copy-start = (bf16[384,3072]{1,0:T(8,128)(2,1)S(1)}, bf16[384,3072]{1,0:T(8,128)(2,1)}, u32[]{:S(2)}) copy-start(bf16[384,3072]{1,0:T(8,128)(2,1)} %param.13) | copy-start | bytes 7077892
  8.0 0.7 copy-start.4
  13.8 16.9 %copy-start.2 = (bf16[256,384]{1,0:T(8,128)(2,1)S(1)}, bf16[256,384]{1,0:T(8,128)(2,1)}, u32[]{:S(2)}) copy-start(bf16[256,384]{1,0:T(8,128)(2,1)} %param.10) | copy-start | bytes 589828
  13.8 16.9 %copy-start.3 = (bf16[256,384]{1,0:T(8,128)(2,1)S(1)}, bf16[256,384]{1,0:T(8,128)(2,1)}, u32[]{:S(2)}) copy-start(bf16[256,384]{1,0:T(8,128)(2,1)} %param.9) | copy-start | bytes 589828
  13.8 295.5 %all-to-all-start = ((bf16[2,64,1,64,384]{4,3,0,2,1:T(8,128)(2,1)}), bf16[2,64,1,64,384]{4,3,0,2,1:T(8,128)(2,1)}, u32[]{:S(2)}, u32[]{:S(2)}) async-start(bf16[2,64,1,64,384]{4,3,0,2,1:T(8,128)(2,1)} %bitcast.86), calls=%async_computation | async-start | bytes 12582912 | tf_op jit(solution)/shard_map/all_to_all | solution.py:97
  30.7 428.5 %reduce-scatter.4.cloned.1.call-start = ((), (), s32[]{:S(2)}) async-start(), calls=%async_computation.2 | async-start | bytes 1769472
  30.9 151.2 %collective-permute-start = (bf16[2,256,384]{2,1,0:T(8,128)(2,1)S(1)}, bf16[2,256,384]{2,1,0:T(8,128)(2,1)}, u32[]{:S(2)}, u32[]{:S(2)}) collective-permute-start(bf16[2,256,384]{2,1,0:T(8,128)(2,1)S(1)} %pad_maximum_fusion), channel_id=1, source_target_pairs={{0,32},{8,40},{16,48},{24,56},{32,64},{40,72},{48,80},{56,88},{64,... | collective-permute-start | bytes 1179656 | tf_op jit(solution)/shard_map/ppermute | solution.py:17
  38.0 190.3 %collective-permute-start.1 = (bf16[2,256,384]{2,1,0:T(8,128)(2,1)S(1)}, bf16[2,256,384]{2,1,0:T(8,128)(2,1)}, u32[]{:S(2)}, u32[]{:S(2)}) collective-permute-start(bf16[2,256,384]{2,1,0:T(8,128)(2,1)S(1)} %pad_maximum_fusion), channel_id=1, source_target_pairs={{0,24},{8,32},{16,40},{24,48},{32,56},{40,64},{48,72},{56,80},{64,... | collective-permute-start | bytes 1179656 | tf_op jit(solution)/shard_map/ppermute | solution.py:17
  41.4 226.1 %collective-permute-start.2 = (bf16[2,256,384]{2,1,0:T(8,128)(2,1)S(1)}, bf16[2,256,384]{2,1,0:T(8,128)(2,1)}, u32[]{:S(2)}, u32[]{:S(2)}) collective-permute-start(bf16[2,256,384]{2,1,0:T(8,128)(2,1)S(1)} %pad_maximum_fusion), channel_id=1, source_target_pairs={{0,16},{8,24},{16,32},{24,40},{32,48},{40,56},{48,64},{56,72},{64,... | collective-permute-start | bytes 1179656 | tf_op jit(solution)/shard_map/ppermute | solution.py:17
  45.7 230.2 %collective-permute-start.3 = (bf16[2,256,384]{2,1,0:T(8,128)(2,1)S(1)}, bf16[2,256,384]{2,1,0:T(8,128)(2,1)}, u32[]{:S(2)}, u32[]{:S(2)}) collective-permute-start(bf16[2,256,384]{2,1,0:T(8,128)(2,1)S(1)} %pad_maximum_fusion), channel_id=1, source_target_pairs={{0,8},{8,16},{16,24},{24,32},{32,40},{40,48},{48,56},{56,64},{64,7... | collective-permute-start | bytes 1179656 | tf_op jit(solution)/shard_map/ppermute | solution.py:17
  48.3 230.2 %collective-permute-start.4 = (bf16[2,256,384]{2,1,0:T(8,128)(2,1)S(1)}, bf16[2,256,384]{2,1,0:T(8,128)(2,1)S(1)}, u32[]{:S(2)}, u32[]{:S(2)}) collective-permute-start(bf16[2,256,384]{2,1,0:T(8,128)(2,1)S(1)} %pad_maximum_fusion), channel_id=1, source_target_pairs={{8,0},{16,8},{24,16},{32,24},{40,32},{48,40},{56,48},{64,56},{72,6... | collective-permute-start | bytes 1179656 | tf_op jit(solution)/shard_map/ppermute | solution.py:17
  182.0 97.2 %collective-permute-start.5 = (bf16[2,256,384]{2,1,0:T(8,128)(2,1)S(1)}, bf16[2,256,384]{2,1,0:T(8,128)(2,1)S(1)}, u32[]{:S(2)}, u32[]{:S(2)}) collective-permute-start(bf16[2,256,384]{2,1,0:T(8,128)(2,1)S(1)} %pad_maximum_fusion), channel_id=1, source_target_pairs={{16,0},{24,8},{32,16},{40,24},{48,32},{56,40},{64,48},{72,56},{80,... | collective-permute-start | bytes 1179656 | tf_op jit(solution)/shard_map/ppermute | solution.py:17
  228.3 51.8 %collective-permute-start.6 = (bf16[2,256,384]{2,1,0:T(8,128)(2,1)S(1)}, bf16[2,256,384]{2,1,0:T(8,128)(2,1)S(1)}, u32[]{:S(2)}, u32[]{:S(2)}) collective-permute-start(bf16[2,256,384]{2,1,0:T(8,128)(2,1)S(1)} %pad_maximum_fusion), channel_id=1, source_target_pairs={{24,0},{32,8},{40,16},{48,24},{56,32},{64,40},{72,48},{80,56},{88,... | collective-permute-start | bytes 1179656 | tf_op jit(solution)/shard_map/ppermute | solution.py:17
  267.5 41.0 %collective-permute-start.7 = (bf16[2,256,384]{2,1,0:T(8,128)(2,1)S(1)}, bf16[2,256,384]{2,1,0:T(8,128)(2,1)S(1)}, u32[]{:S(2)}, u32[]{:S(2)}) collective-permute-start(bf16[2,256,384]{2,1,0:T(8,128)(2,1)S(1)} %pad_maximum_fusion), channel_id=1, source_target_pairs={{32,0},{40,8},{48,16},{56,24},{64,32},{72,40},{80,48},{88,56},{96,... | collective-permute-start | bytes 1179656 | tf_op jit(solution)/shard_map/ppermute | solution.py:17
  321.1 4.0 copy-start.5
  341.0 2.0 copy-start.1
  361.3 2.0 copy-start.1
  381.6 2.0 copy-start.1
Sparse Core Ops, SparseCore 0:
  391.8 67.3 reduce-scatter.3
where the time goes:
time: 469 us; the launch traced here: 468 us
  waiting for transfers between devices  305 us (65%)
  local copies, waits for them, and re-layouts  65.7 us (14%)
  starting transfers between devices  42.1 us (9%)
  matrix products  22 us (5%)
  other arithmetic  16.9 us (4%)
  between operations  13.6 us (3%)
    ppermute x8, waiting for transfers between devices, from_behind(): lax.ppermute(value, axis, [(source, source + steps) for source in range(f...  238 us
    unnamed x2, waiting for transfers between devices  67.5 us
    ppermute x8, starting transfers between devices, from_behind(): lax.ppermute(value, axis, [(source, source + steps) for source in range(f...  25.2 us
    all_to_all x1, starting transfers between devices, shards(): lax.all_to_all(stretched[:, local_pick], 'seq', split_axis=1, concat_axis...  16.9 us
    unnamed x20, local copies, waits for them, and re-layouts  14.9 us
    slice x3, local copies, waits for them, and re-layouts, shot_part(): window[1]  10.8 us
    slice x3, local copies, waits for them, and re-layouts, routed_part(): routed_values = lax.dynamic_slice(routed[1], corner, extent)  10.4 us
    reduce_sum x3, other arithmetic, shot_part(): mass = jnp.sum(weights, axis=1)  9.55 us
  transfers between devices with their start and end apart: 10, of which 6 were waited for; matrix products, arithmetic and copies ran while one was open for 3% of the time, Pallas kernels for 0%

commit v1 on v0

v1 whole, which is shorter than its diff:
```python
import functools
import math

import jax
import jax.numpy as jnp
from jax import lax
from jax.experimental import pallas as pl
from jax.experimental.pallas import tpu as pltpu
from jax.sharding import PartitionSpec as P

D = 128
ROWS = 256
STRETCH = 64
ROUTES = 8
SEQ = 64
PER = ROWS // STRETCH
NY = 8
COLS = 6
TOKENS = SEQ * ROWS
HALF = 4 * ROWS
SUB = 128
REACH = 1024
WINDOW = SUB + 2 * REACH
NEGATIVE = -1e30
FACTOR = D ** -0.5 * math.log2(math.e)
NT = (((1,), (1,)), ((), ()))
RIGHT, LEFT = 0, 1


def kernel(q_ref, k_ref, v_ref, ids_ref, routes_ref, w_ref, out_ref,
           kbuf, vbuf, qbuf, att, gbuf, wbuf, top_s, mass_s, acc_s,
           qs, qr, ring_s, ring_r, sib_s, sib_r, w_s, w_r, back_s, back_r,
           xs, xr, x2s, x2r, xsib_s, xsib_r):
    p = lax.axis_index("seq")
    hd = lax.axis_index("head")
    z, y = p // NY, p % NY
    x, c = hd // 2, hd % 2
    sibling = (p, 2 * x + 1 - c)
    bufs = (kbuf, vbuf)

    def remote(src, dst, send, recv, device):
        return pltpu.make_async_remote_copy(
            src_ref=src, dst_ref=dst, send_sem=send, recv_sem=recv,
            device_id=device, device_id_type=pl.DeviceIdType.MESH)

    def arrived(ref, sem):
        pltpu.make_async_copy(ref, ref, sem).wait()

    def sent(ref, sem):
        pltpu.make_async_copy(ref, ref, sem).wait()

    barrier = pltpu.get_barrier_semaphore()
    peers = [sibling]
    for d in range(1, NY):
        there = z * NY + (y + d) % NY
        peers += [(there, hd), (there, 2 * x + 1 - c)]
    zr, zl = (z + 1) % 8 * NY + y, (z + 7) % 8 * NY + y
    peers += [(zr, hd), (zl, hd)]
    for d in range(1, 4):
        xo = (x + d) % 4
        peers += [(p, 2 * xo), (p, 2 * xo + 1)]
    for device in peers:
        pl.semaphore_signal(barrier, inc=1, device_id=device,
                            device_id_type=pl.DeviceIdType.MESH)
    pl.semaphore_wait(barrier, len(peers))

    core = y // 4
    row0, q0 = p * PER, y % 4 * PER
    for t, (src, dst, at) in enumerate(((k_ref, kbuf, row0), (v_ref, vbuf, row0), (q_ref, qbuf, q0))):
        for i in range(3):
            h = 3 * c + i
            part = src.at[:, :, i * D:(i + 1) * D]
            own = jnp.logical_and(h == y, core == c)

            @pl.when(jnp.logical_not(own))
            def _():
                remote(part, dst.at[pl.ds(at, PER)], qs.at[i, t], qr.at[y % 4, t],
                       (z * NY + h, 2 * x + core)).start()

            @pl.when(own)
            def _():
                pltpu.make_async_copy(part, dst.at[pl.ds(at, PER)], qr.at[y % 4, t]).start()

    w_here = wbuf.at[pl.ds(pl.multiple_of(hd * 384, 384), 384)]
    for d in range(1, 8):
        other = (hd + d) % 8
        remote(w_ref.at[:, pl.ds(pl.multiple_of(other * 384, 384), 384)], w_here,
               w_s.at[d], w_r.at[d], (p, other)).start()
    w_own = pltpu.make_async_copy(
        w_ref.at[:, pl.ds(pl.multiple_of(hd * 384, 384), 384)], w_here, w_s.at[0])
    w_own.start()

    def half(t, row, core_of):
        return bufs[t].at[pl.ds((row * 2 + core_of) * (HALF // STRETCH), HALF // STRETCH)]

    def to_sibling(t, o, row):
        ref = half(t, row, c)
        return remote(ref, ref, sib_s.at[o, t], sib_r.at[o, t], sibling)

    def hop(t, way, step, row):
        ref = half(t, row, c)
        return remote(ref, ref, ring_s.at[way, step, t], ring_r.at[way, step, t],
                      (zr if way == RIGHT else zl, hd))

    def origin(way, step):
        return (z + 8 - 1 - step) % 8 if way == RIGHT else (z + 1 + step) % 8

    def slot(way, step):
        return 1 + 2 * step + way if step < 3 else 7

    def goes(t, way, step):
        return step < 3 or t == way

    def shot(b):
        start = (z * 2 + c) * (HALF // SUB) + b
        pieces = [(start + n + TOKENS // SUB - REACH // SUB) % (TOKENS // SUB)
                  for n in range(WINDOW // SUB)]
        rows = [pl.ds(n * (SUB // STRETCH), SUB // STRETCH) for n in pieces]
        at = pl.ds(pl.multiple_of(b * SUB, SUB), SUB)
        q = qbuf[pl.ds(b * (SUB // STRETCH), SUB // STRETCH)].reshape(SUB, D)
        mine = jnp.broadcast_to(ids_ref[pl.ds(start, 1), :], (SUB, SUB)).T
        scores = []
        peak = None
        for n, r in zip(pieces, rows):
            s = lax.dot_general(q, kbuf[r].reshape(SUB, D), NT, preferred_element_type=jnp.float32)
            s = jnp.where(mine == ids_ref[pl.ds(n, 1), :], s, NEGATIVE)
            peak = s if peak is None else jnp.maximum(peak, s)
            scores.append(s)
        top = jnp.max(peak, axis=1, keepdims=True)
        total = None
        acc = None
        for s, r in zip(scores, rows):
            e = jnp.exp2((s - top) * FACTOR)
            total = e if total is None else total + e
            one = jnp.dot(e.astype(jnp.bfloat16), vbuf[r].reshape(SUB, D), preferred_element_type=jnp.float32)
            acc = one if acc is None else acc + one
        mass = jnp.sum(total, axis=1, keepdims=True)
        top_s[at, :] = jnp.broadcast_to(top, (SUB, D))
        mass_s[at, :] = jnp.broadcast_to(mass, (SUB, D))
        acc_s[at, :] = acc

    def routed(b, g):
        at = pl.ds(pl.multiple_of(b * ROWS + g * STRETCH, STRETCH), STRETCH)
        stretch = (z * 2 + c) * 16 + b * 4 + g
        rows = [routes_ref[j, stretch] for j in range(ROUTES)]
        keys = jnp.concatenate([kbuf[r] for r in rows], axis=0)
        s = lax.dot_general(qbuf[b * PER + g], keys, NT, preferred_element_type=jnp.float32)
        before = top_s[at, :]
        top = jnp.maximum(before, jnp.max(s, axis=1, keepdims=True))
        e = jnp.exp2((s - top[:, :1]) * FACTOR)
        keep = jnp.exp2((before - top) * FACTOR)
        mass = keep * mass_s[at, :] + jnp.sum(e, axis=1, keepdims=True)
        vals = jnp.concatenate([vbuf[r] for r in rows], axis=0)
        summed = keep * acc_s[at, :] + jnp.dot(e.astype(jnp.bfloat16), vals,
                                               preferred_element_type=jnp.float32)
        att[b, pl.ds(pl.multiple_of(g * STRETCH, STRETCH), STRETCH), :] = (
            summed / mass).astype(jnp.bfloat16)

    def back(b):
        to = 4 * c + b
        piece = gbuf.at[6 * x + y]
        device = (z * NY + to, 2 * x + y // 3)
        own = jnp.logical_and(to == y, y // 3 == c)
        return piece, device, own

    @pl.when(y < COLS)
    def _():
        for t in range(2):
            for n in range(4):
                arrived(kbuf.at[pl.ds(0, PER)], qr.at[n, t])
            hop(t, RIGHT, 0, z).start()
            hop(t, LEFT, 0, z).start()
            to_sibling(t, 0, z).start()
        for n in range(4):
            arrived(qbuf.at[pl.ds(0, PER)], qr.at[n, 2])

        def pass_on(step):
            for t in range(2):
                for way in (RIGHT, LEFT):
                    if not goes(t, way, step):
                        continue
                    row = origin(way, step)
                    arrived(half(t, row, c), ring_r.at[way, step, t])
                    if step < 3 and goes(t, way, step + 1):
                        hop(t, way, step + 1, row).start()
                    to_sibling(t, slot(way, step), row).start()

        def from_sibling(o, row):
            for t in range(2):
                arrived(half(t, row, 1 - c), sib_r.at[o, t])

        def shots(first, last):
            pl.loop(first, last)(shot)

        pass_on(0)
        from_sibling(0, z)
        from_sibling(slot(RIGHT, 0), origin(RIGHT, 0))
        from_sibling(slot(LEFT, 0), origin(LEFT, 0))
        shots(0, 3)
        pass_on(1)
        shots(3, 6)
        pass_on(2)
        shots(6, 8)
        pass_on(3)
        for step in (1, 2):
            for way in (RIGHT, LEFT):
                from_sibling(slot(way, step), origin(way, step))
        from_sibling(7, origin(RIGHT, 3))

        for b in range(4):
            pl.loop(0, 4)(functools.partial(routed, b))
            piece, device, own = back(b)

            @pl.when(jnp.logical_not(own))
            def _():
                remote(att.at[b], piece, back_s.at[b], back_r.at[y % 3], device).start()

            @pl.when(own)
            def _():
                pltpu.make_async_copy(att.at[b], piece, back_r.at[y % 3]).start()

    xright, xleft = (p, (x + 1) % 4 * 2 + c), (p, (x + 3) % 4 * 2 + c)
    beside = (xright, xleft)
    top_rows, low_rows = pl.ds(0, ROWS // 2), pl.ds(ROWS // 2, ROWS // 2)
    parts = (top_rows, low_rows)
    sends = []

    def go(copy):
        copy.start()
        sends.append(copy)

    for i in range(3):
        ref = gbuf.at[3 * hd + i]
        arrived(ref, back_r.at[i])
        for way in (RIGHT, LEFT):
            go(remote(ref, ref, xs.at[way, i], xr.at[way, i], beside[way]))
        go(remote(ref, ref, xsib_s.at[0, i], xsib_r.at[0, i], sibling))
    for i in range(3):
        for way in (RIGHT, LEFT):
            xo = (x + 3) % 4 if way == RIGHT else (x + 1) % 4
            ref = gbuf.at[3 * (2 * xo + c) + i]
            arrived(ref, xr.at[way, i])
            cut = gbuf.at[3 * (2 * xo + c) + i, parts[way]]
            go(remote(cut, cut, x2s.at[way, i], x2r.at[way, i], beside[way]))
            go(remote(ref, ref, xsib_s.at[1 + way, i], xsib_r.at[1 + way, i], sibling))
    far = (x + 2) % 4
    for i in range(3):
        for way in (RIGHT, LEFT):
            cut = gbuf.at[3 * (2 * far + c) + i, parts[way]]
            arrived(cut, x2r.at[way, i])
            go(remote(cut, cut, xsib_s.at[3 + way, i], xsib_r.at[3 + way, i], sibling))
    for i in range(3):
        for o, xo in ((0, x), (1, (x + 3) % 4), (2, (x + 1) % 4)):
            arrived(gbuf.at[3 * (2 * xo + 1 - c) + i], xsib_r.at[o, i])
        for way in (RIGHT, LEFT):
            arrived(gbuf.at[3 * (2 * far + 1 - c) + i, parts[way]], xsib_r.at[3 + way, i])
    w_own.wait()
    for d in range(1, 8):
        arrived(w_here, w_r.at[d])

    left = jnp.concatenate([gbuf[n] for n in range(24)], axis=1)
    out_ref[...] = jnp.dot(left, wbuf[...], preferred_element_type=jnp.float32).astype(jnp.bfloat16)

    for copy in sends:
        copy.wait_send()
    for d in range(1, 8):
        sent(w_here, w_s.at[d])
    for t in range(3):
        for i in range(3):
            own = jnp.logical_and(3 * c + i == y, core == c)

            @pl.when(jnp.logical_not(own))
            def _():
                sent(qbuf.at[pl.ds(0, PER)], qs.at[i, t])

    @pl.when(y < COLS)
    def _():
        for t in range(2):
            to_sibling(t, 0, z).wait_send()
            for step in range(4):
                for way in (RIGHT, LEFT):
                    if goes(t, way, step):
                        hop(t, way, step, z).wait_send()
                        to_sibling(t, slot(way, step), z).wait_send()
        for b in range(4):
            piece, device, own = back(b)

            @pl.when(jnp.logical_not(own))
            def _():
                sent(att.at[b], back_s.at[b])


def shards(query, keys, values, shot_ids, routes, out_weight):
    vmem, hbm = pl.BlockSpec(memory_space=pltpu.VMEM), pl.BlockSpec(memory_space=pl.ANY)
    dma = pltpu.SemaphoreType.DMA
    return pl.pallas_call(
        kernel,
        out_shape=jax.ShapeDtypeStruct((ROWS, 384), jnp.bfloat16),
        in_specs=[hbm, hbm, hbm, vmem, pl.BlockSpec(memory_space=pltpu.SMEM), hbm],
        out_specs=vmem,
        scratch_shapes=[
            pltpu.VMEM((TOKENS // STRETCH, STRETCH, D), jnp.bfloat16),
            pltpu.VMEM((TOKENS // STRETCH, STRETCH, D), jnp.bfloat16),
            pltpu.VMEM((HALF // STRETCH, STRETCH, D), jnp.bfloat16),
            pltpu.VMEM((4, ROWS, D), jnp.bfloat16),
            pltpu.VMEM((24, ROWS, D), jnp.bfloat16),
            pltpu.VMEM((3072, 384), jnp.bfloat16),
            pltpu.VMEM((HALF, D), jnp.float32),
            pltpu.VMEM((HALF, D), jnp.float32),
            pltpu.VMEM((HALF, D), jnp.float32),
            dma((3, 3)), dma((4, 3)),
            dma((2, 4, 2)), dma((2, 4, 2)),
            dma((8, 2)), dma((8, 2)),
            dma((8,)), dma((8,)),
            dma((4,)), dma((3,)),
            dma((2, 3)), dma((2, 3)),
            dma((2, 3)), dma((2, 3)),
            dma((5, 3)), dma((5, 3)),
        ],
        compiler_params=pltpu.CompilerParams(
            collective_id=0, has_side_effects=True, vmem_limit_bytes=48 * 1024 * 1024),
        cost_estimate=pl.CostEstimate(
            flops=2_400_000_000, bytes_accessed=4_000_000, transcendentals=3_000_000),
    )(*(a.reshape(PER, STRETCH, 384) for a in (query, keys, values)), shot_ids.reshape(TOKENS // SUB, SUB), routes.T, out_weight)


def solution(mesh):
    placed = (P("seq", "head"), P("seq", "head"), P("seq", "head"), P(), P(), P("head", None))
    return jax.shard_map(
        shards, mesh=mesh, in_specs=placed, out_specs=P("seq", "head"), check_vma=False
    )
```

time: 469 us -> 98.5 us (0.21)
  the two profiles are of different devices: /device:TPU:8 before, /device:TPU:57 now
where the time goes in v1:
time: 98.5 us; the launch traced here: 98.2 us
  Pallas kernels  91.5 us (93%)
  local copies, waits for them, and re-layouts  6.66 us (7%)
    pallas_call x1, Pallas kernels, shards(): pl.pallas_call(kernel, out_shape=jax.ShapeDtypeStruct((ROWS, 384), jnp.bf...  91.5 us
    unnamed x13, local copies, waits for them, and re-layouts  6.66 us

profile of v1, /device:TPU:57, one launch (start us, length us, event | category | flops | bytes accessed | tf_op | source)
XLA Modules:
  0.0 98.2 jit_solution(12437098297612025079)
XLA Ops:
  0.0 0.0 copy-start
  0.0 1.7 %copy-done = bf16[384,3072]{1,0:T(8,128)(2,1)S(1)} copy-done((bf16[384,3072]{1,0:T(8,128)(2,1)S(1)}, bf16[384,3072]{1,0:T(8,128)(2,1)}, u32[]{:S(2)}) %copy-start) | copy-done | bytes 2359320
  1.7 0.0 copy-start.1
  1.7 0.9 copy-done.1
  2.6 0.0 copy-start.2
  2.6 0.9 copy-done.2
  3.5 0.0 copy-start.3
  3.5 0.9 copy-done.3
  4.4 0.0 copy-start.4
  4.5 0.8 copy-done.4
  5.3 0.0 copy-start.5
  5.3 0.7 copy-done.5
  6.0 91.5 %shard_map.64 = bf16[256,384]{1,0:T(8,128)(2,1)S(1)} custom-call(bf16[4,64,384]{2,1,0:T(8,128)(2,1)S(1)} %bitcast.5, bf16[4,64,384]{2,1,0:T(8,128)(2,1)S(1)} %bitcast.6, bf16[4,64,384]{2,1,0:T(8,128)(2,1)S(1)} %bitcast.7, s32[128,128]{1,0:T(8,128)S(1)} %bitcast.8, s32[8,256]{1,0:T(8,128)S(1)} %bitcast.9, bf16[384,3072]{1,0:T(8,128)(2,1)S(1)} %copy-done), custom_call_target="tpu_custom_call" | custom-call | flops 2400000000 | bytes 4000000 | tf_op jit(solution)/shard_map/pallas_call | solution.py:296
  97.5 0.7 copy.8
Async XLA Ops:
  0.0 1.7 %copy-start = (bf16[384,3072]{1,0:T(8,128)(2,1)S(1)}, bf16[384,3072]{1,0:T(8,128)(2,1)}, u32[]{:S(2)}) copy-start(bf16[384,3072]{1,0:T(8,128)(2,1)} %w_ref.1) | copy-start | bytes 7077892
  1.7 0.9 copy-start.1
  2.6 0.9 copy-start.2
  3.5 0.9 copy-start.3
  4.4 0.8 copy-start.4
  5.3 0.7 copy-start.5

commit v2 on v1

v2 whole, which is shorter than its diff:
```python
import math

import jax
import jax.numpy as jnp
from jax import lax
from jax.experimental import pallas as pl
from jax.experimental.pallas import tpu as pltpu
from jax.sharding import PartitionSpec as P

D = 128
ROWS = 256
STRETCH = 64
ROUTES = 8
SEQ = 64
PER = ROWS // STRETCH
NY = 8
SPARE = 3
TOKENS = SEQ * ROWS
HALF = 4 * ROWS
SUB = 128
REACH = 1024
WINDOW = SUB + 2 * REACH
NEGATIVE = -1e30
FACTOR = D ** -0.5 * math.log2(math.e)
NT = (((1,), (1,)), ((), ()))
RIGHT, LEFT = 0, 1


def kernel(q_ref, k_ref, v_ref, ids_hbm, routes_hbm, w_ref, out_ref,
           ids_ref, routes_ref, small, kv, qbuf, att, gbuf, wbuf, total, top_s, mass_s, acc_s,
           qs, qr, ring_s, ring_r, sib_s, sib_r, hand_s, hand_r, spare_s, w_s, w_r, back_s, back_r,
           xs, xr, x2s, x2r, xsib_s, xsib_r):
    p = lax.axis_index("seq")
    hd = lax.axis_index("head")
    z, y = p // NY, p % NY
    x, c = hd // 2, hd % 2
    sibling = (p, 2 * x + 1 - c)

    def remote(src, dst, send, recv, device):
        return pltpu.make_async_remote_copy(
            src_ref=src, dst_ref=dst, send_sem=send, recv_sem=recv,
            device_id=device, device_id_type=pl.DeviceIdType.MESH)

    def arrived(ref, sem):
        pltpu.make_async_copy(ref, ref, sem).wait()

    def sent(ref, sem):
        pltpu.make_async_copy(ref, ref, sem).wait()

    ids_copy = pltpu.make_async_copy(ids_hbm, ids_ref, small.at[0])
    routes_copy = pltpu.make_async_copy(routes_hbm, routes_ref, small.at[1])
    ids_copy.start()
    routes_copy.start()

    barrier = pltpu.get_barrier_semaphore()
    peers = [sibling]
    for d in range(1, NY):
        there = z * NY + (y + d) % NY
        peers += [(there, hd), (there, 2 * x + 1 - c)]
    zr, zl = (z + 1) % 8 * NY + y, (z + 7) % 8 * NY + y
    peers += [(zr, hd), (zl, hd)]
    for d in range(1, 4):
        xo = (x + d) % 4
        peers += [(p, 2 * xo), (p, 2 * xo + 1)]
    for device in peers:
        pl.semaphore_signal(barrier, inc=1, device_id=device,
                            device_id_type=pl.DeviceIdType.MESH)
    pl.semaphore_wait(barrier, len(peers))

    core = y // 4
    row0, q0 = p * PER, y % 4 * PER
    own_k = kv.at[pl.ds(row0, PER), :, 0:D]
    own_v = kv.at[pl.ds(row0, PER), :, D:2 * D]
    own_q = qbuf.at[pl.ds(q0, PER)]
    turned = (y + 10 - 4 * c) % 8 // 4

    def to_column(n, t, src, dst):
        i = n + turned * (2 - 2 * n)
        h = 4 * c + i
        own = h == y
        part = src.at[:, :, pl.ds(pl.multiple_of(i * D, D), D)]

        @pl.when(jnp.logical_not(own))
        def _():
            remote(part, dst, qs.at[n, t], qr.at[y % 4, t], (z * NY + h, 2 * x + core)).start()

        @pl.when(own)
        def _():
            pltpu.make_async_copy(part, dst, qr.at[y % 4, t]).start()

    def left_for_column(n, t):
        h = 4 * c + n + turned * (2 - 2 * n)

        @pl.when(h != y)
        def _():
            sent(qbuf.at[pl.ds(0, PER)], qs.at[n, t])

    def queries_to_columns():
        for n in range(3):
            to_column(n, 2, q_ref, own_q)

    for n in range(3):
        to_column(n, 0, k_ref, own_k)
        to_column(n, 1, v_ref, own_v)

    w_here = wbuf.at[pl.ds(3 * hd, 3)]

    def w_part(of):
        return w_ref.at[:, :, pl.ds(pl.multiple_of(of * 384, 384), 384)]

    for d in range(1, 8):
        other = (hd + d) % 8
        remote(w_part(other), w_here, w_s.at[d], w_r.at[d], (p, other)).start()
    w_own = pltpu.make_async_copy(w_part(hd), w_here, w_s.at[0])
    w_own.start()

    def nth(k, core_of):
        return (y + 2 * ((y // 4 + core_of) % 2) + (0, 1, 3, 2)[k]) % 4

    def piece_of(row, core_of, n):
        return kv.at[pl.ds((row * NY + 4 * core_of + n) * PER, PER)]

    def half_of(row, core_of):
        return kv.at[pl.ds((row * NY + 4 * core_of) * PER, 4 * PER)]

    def to_sibling(o, row, n):
        ref = piece_of(row, c, n)
        return remote(ref, ref, sib_s.at[o], sib_r.at[o], sibling)

    def hop(way, step, ref, n):
        return remote(ref, ref, ring_s.at[way, step, n], ring_r.at[way, step, n],
                      (zr if way == RIGHT else zl, hd))

    lean = jnp.logical_xor(core == c, y % 4 == 0)

    def in_ring(n):
        return jnp.logical_not(jnp.logical_and(lean, n == SPARE))

    def origin(way, step):
        return (z + 8 - 1 - step) % 8 if way == RIGHT else (z + 1 + step) % 8

    def slot(way, step):
        return 1 + 2 * step + way if step < 3 else 7

    def goes(k, way, step):
        return step < 3 or k // 2 == way

    def shot(b):
        start = (z * 2 + c) * (HALF // SUB) + b
        pieces = [(start + n + TOKENS // SUB - REACH // SUB) % (TOKENS // SUB)
                  for n in range(WINDOW // SUB)]
        rows = [pl.ds(n * (SUB // STRETCH), SUB // STRETCH) for n in pieces]
        at = pl.ds(pl.multiple_of(b * SUB, SUB), SUB)
        q = qbuf[pl.ds(b * (SUB // STRETCH), SUB // STRETCH)].reshape(SUB, D)
        mine = jnp.broadcast_to(ids_ref[pl.ds(start, 1), :], (SUB, SUB)).T
        scores = []
        peak = None
        for n, r in zip(pieces, rows):
            s = lax.dot_general(q, kv[r, :, 0:D].reshape(SUB, D), NT, preferred_element_type=jnp.float32)
            s = jnp.where(mine == ids_ref[pl.ds(n, 1), :], s, NEGATIVE)
            peak = s if peak is None else jnp.maximum(peak, s)
            scores.append(s)
        top = jnp.max(peak, axis=1, keepdims=True)
        added = None
        acc = None
        for s, r in zip(scores, rows):
            e = jnp.exp2((s - top) * FACTOR)
            added = e if added is None else added + e
            one = jnp.dot(e.astype(jnp.bfloat16), kv[r, :, D:2 * D].reshape(SUB, D), preferred_element_type=jnp.float32)
            acc = one if acc is None else acc + one
        mass = jnp.sum(added, axis=1, keepdims=True)
        top_s[at, :] = jnp.broadcast_to(top, (SUB, D))
        mass_s[at, :] = jnp.broadcast_to(mass, (SUB, D))
        acc_s[at, :] = acc

    def routed(b):
        ats = [pl.ds(pl.multiple_of(b * ROWS, ROWS) + g * STRETCH, STRETCH) for g in range(PER)]
        stretch = (z * 2 + c) * 16 + b * PER
        rows = [[routes_ref[j, stretch + g] for j in range(ROUTES)] for g in range(PER)]
        scores = []
        for g in range(PER):
            keys = jnp.concatenate([kv[r, :, 0:D] for r in rows[g]], axis=0)
            scores.append(lax.dot_general(qbuf[b * PER + g], keys, NT,
                                          preferred_element_type=jnp.float32))
        before = [top_s[at, :] for at in ats]
        tops = [jnp.maximum(t, jnp.max(s, axis=1, keepdims=True)) for t, s in zip(before, scores)]
        exps = [jnp.exp2((s - t[:, :1]) * FACTOR) for s, t in zip(scores, tops)]
        keeps = [jnp.exp2((o - t) * FACTOR) for o, t in zip(before, tops)]
        sums = []
        for g in range(PER):
            vals = jnp.concatenate([kv[r, :, D:2 * D] for r in rows[g]], axis=0)
            sums.append(jnp.dot(exps[g].astype(jnp.bfloat16), vals,
                                preferred_element_type=jnp.float32))
        for g in range(PER):
            mass = keeps[g] * mass_s[ats[g], :] + jnp.sum(exps[g], axis=1, keepdims=True)
            summed = keeps[g] * acc_s[ats[g], :] + sums[g]
            att[b, g * STRETCH:(g + 1) * STRETCH, :] = (summed / mass).astype(jnp.bfloat16)

    def back(b):
        to = 4 * c + b
        return gbuf.at[6 * x + 3 * core + y % 4], (z * NY + to, 2 * x + core), to == y

    ids_copy.wait()
    routes_copy.wait()

    @pl.when(y % 4 < SPARE)
    def _():
        def own(k):
            n = nth(k, c)
            ref = piece_of(z, c, n)
            for t in range(2):
                arrived(qbuf.at[pl.ds(0, PER)], qr.at[n, t])

            @pl.when(in_ring(n))
            def _():
                hop(RIGHT, 0, ref, n).start()
                hop(LEFT, 0, ref, n).start()

            to_sibling(0, z, n).start()

        def pass_on(step, k):
            n = nth(k, c)

            @pl.when(in_ring(n))
            def _():
                for way in (RIGHT, LEFT):
                    if goes(k, way, step):
                        row = origin(way, step)
                        ref = piece_of(row, c, n)
                        arrived(ref, ring_r.at[way, step, n])
                        if step < 3 and goes(k, way, step + 1):
                            hop(way, step + 1, ref, n).start()
                        to_sibling(slot(way, step), row, n).start()

        def handed(step):
            @pl.when(lean)
            def _():
                for way in (RIGHT, LEFT)[:2 if step < 3 else 1]:
                    row = origin(way, step)
                    arrived(piece_of(row, c, SPARE), hand_r.at[slot(way, step)])
                    to_sibling(slot(way, step), row, SPARE).start()

        def from_sibling(o, row):
            arrived(half_of(row, 1 - c), sib_r.at[o])

        own(0)
        own(1)
        pass_on(0, 0)
        own(2)
        pass_on(0, 1)
        own(3)
        queries_to_columns()
        pass_on(0, 2)
        pass_on(0, 3)
        handed(0)
        for n in range(4):
            arrived(qbuf.at[pl.ds(0, PER)], qr.at[n, 2])
        from_sibling(0, z)
        from_sibling(slot(RIGHT, 0), origin(RIGHT, 0))
        from_sibling(slot(LEFT, 0), origin(LEFT, 0))
        for k in range(4):
            pl.loop(2 * k, 2 * k + 2)(shot)
            pass_on(1, k)
        handed(1)
        for step in (2, 3):
            for k in range(4):
                pass_on(step, k)
            handed(step)
        for step in (1, 2):
            for way in (RIGHT, LEFT):
                from_sibling(slot(way, step), origin(way, step))
        from_sibling(7, origin(RIGHT, 3))

        for k in range(4):
            b = (k + y) % 4
            routed(b)
            piece, device, mine = back(b)

            @pl.when(jnp.logical_not(mine))
            def _():
                remote(att.at[b], piece, back_s.at[k], back_r.at[y % 4], device).start()

            @pl.when(mine)
            def _():
                pltpu.make_async_copy(att.at[b], piece, back_r.at[y % 4]).start()

    paired = jnp.where(core == c, 1, 0)

    def served(j):
        return paired * (2 - j), (y + 9 - paired * (2 + j)) % NY

    def each(fn):
        fn(0)

        @pl.when(paired == 1)
        def _():
            fn(1)

    def spare_piece(row, j):
        return kv.at[pl.ds((row * NY + j) * PER, PER)]

    def spare_goes(j, way, step):
        return step < 3 or j == way

    def hand(o, row, j):
        return remote(spare_piece(row, j), kv.at[pl.ds((row * NY + y) * PER, PER)],
                      hand_s.at[o, j], hand_r.at[o],
                      (z * NY + served(j)[1], 2 * x + core))

    @pl.when(y % 4 == SPARE)
    def _():
        def fetch(j):
            lanes = pl.ds(pl.multiple_of(served(j)[0] * D, D), D)
            at = pl.ds((z * NY + j) * PER, PER)
            return [pltpu.make_async_copy(src.at[:, :, lanes], kv.at[at, :, t * D:(t + 1) * D],
                                          spare_s.at[j, t]) for t, src in enumerate((k_ref, v_ref))]

        def begin(j):
            for copy in fetch(j):
                copy.start()

        def launch(j):
            for copy in fetch(j):
                copy.wait()
            for way in (RIGHT, LEFT):
                hop(way, 0, spare_piece(z, j), j).start()

        each(begin)
        each(launch)
        for step in range(4):
            def carry(j):
                for way in (RIGHT, LEFT):
                    if spare_goes(j, way, step):
                        row = origin(way, step)
                        arrived(spare_piece(row, j), ring_r.at[way, step, j])
                        if step < 3 and spare_goes(j, way, step + 1):
                            hop(way, step + 1, spare_piece(row, j), j).start()
                        hand(slot(way, step), row, j).start()

            each(carry)
            if step == 0:
                for n in range(3):
                    left_for_column(n, 0)
                    left_for_column(n, 1)
                queries_to_columns()

    xright, xleft = (p, (x + 1) % 4 * 2 + c), (p, (x + 3) % 4 * 2 + c)
    beside = (xright, xleft)
    parts = (pl.ds(0, ROWS // 2), pl.ds(ROWS // 2, ROWS // 2))
    far = (x + 2) % 4
    came = ((x + 3) % 4, (x + 1) % 4)

    def from_columns(i):
        ref = gbuf.at[3 * hd + i]
        arrived(ref, back_r.at[i])
        for way in (RIGHT, LEFT):
            remote(ref, ref, xs.at[way, i], xr.at[way, i], beside[way]).start()
        remote(ref, ref, xsib_s.at[0, i], xsib_r.at[0, i], sibling).start()

    def from_beside(i):
        for way in (RIGHT, LEFT):
            at = 3 * (2 * came[way] + c) + i
            ref, cut = gbuf.at[at], gbuf.at[at, parts[way]]
            arrived(ref, xr.at[way, i])
            remote(cut, cut, x2s.at[way, i], x2r.at[way, i], beside[way]).start()
            remote(ref, ref, xsib_s.at[1 + way, i], xsib_r.at[1 + way, i], sibling).start()

    def from_far(i):
        for way in (RIGHT, LEFT):
            cut = gbuf.at[3 * (2 * far + c) + i, parts[way]]
            arrived(cut, x2r.at[way, i])
            remote(cut, cut, xsib_s.at[3 + way, i], xsib_r.at[3 + way, i], sibling).start()

    def project(core_of, i):
        left = jnp.concatenate([gbuf[3 * (2 * n + core_of) + i] for n in range(4)], axis=1)
        right = jnp.concatenate([wbuf[3 * (2 * n + core_of) + i] for n in range(4)], axis=0)
        total[...] += jnp.dot(left, right, preferred_element_type=jnp.float32)

    def project_own(i):
        project(c, i)

    def project_sibling(i):
        for o, xo in ((0, x), (1, came[RIGHT]), (2, came[LEFT])):
            arrived(gbuf.at[3 * (2 * xo + 1 - c) + i], xsib_r.at[o, i])
        for way in (RIGHT, LEFT):
            arrived(gbuf.at[3 * (2 * far + 1 - c) + i, parts[way]], xsib_r.at[3 + way, i])
        project(1 - c, i)

    def in_turn(n, stage):
        i = (y + 4 - n) % 4

        @pl.when(i < 3)
        def _():
            stage(i)

    total[...] = jnp.zeros((ROWS, 384), jnp.float32)
    w_own.wait()
    for d in range(1, 8):
        arrived(w_here, w_r.at[d])
    for turn in range(7):
        for late, stage in enumerate((from_columns, from_beside, from_far, project_own)):
            if 0 <= turn - late < 4:
                in_turn(turn - late, stage)
    for turn in range(4):
        in_turn(turn, project_sibling)

    out_ref[...] = total[...].astype(jnp.bfloat16)

    for i in range(3):
        for way in (RIGHT, LEFT):
            sent(gbuf.at[0], xs.at[way, i])
            sent(gbuf.at[0, parts[way]], x2s.at[way, i])
            sent(gbuf.at[0, parts[way]], xsib_s.at[3 + way, i])
        for o in range(3):
            sent(gbuf.at[0], xsib_s.at[o, i])
    for d in range(1, 8):
        sent(w_here, w_s.at[d])
    for n in range(3):
        left_for_column(n, 2)

    @pl.when(y % 4 < SPARE)
    def _():
        for n in range(3):
            left_for_column(n, 0)
            left_for_column(n, 1)
        for k in range(4):
            n = nth(k, c)
            ref = piece_of(z, c, n)

            @pl.when(in_ring(n))
            def _():
                for step in range(4):
                    for way in (RIGHT, LEFT):
                        if goes(k, way, step):
                            hop(way, step, ref, n).wait_send()

        for o in range(8):
            sent(half_of(z, c), sib_s.at[o])
        for k in range(4):
            piece, device, mine = back((k + y) % 4)

            @pl.when(jnp.logical_not(mine))
            def _():
                sent(att.at[0], back_s.at[k])

    @pl.when(y % 4 == SPARE)
    def _():
        def gone(j):
            for step in range(4):
                for way in (RIGHT, LEFT):
                    if spare_goes(j, way, step):
                        hop(way, step, spare_piece(z, j), j).wait_send()
                        hand(slot(way, step), z, j).wait_send()

        each(gone)


def shards(query, keys, values, shot_ids, routes, out_weight):
    vmem, hbm = pl.BlockSpec(memory_space=pltpu.VMEM), pl.BlockSpec(memory_space=pl.ANY)
    dma = pltpu.SemaphoreType.DMA
    return pl.pallas_call(
        kernel,
        out_shape=jax.ShapeDtypeStruct((ROWS, 384), jnp.bfloat16),
        in_specs=[hbm] * 6,
        out_specs=vmem,
        scratch_shapes=[
            pltpu.VMEM((TOKENS // SUB, SUB), jnp.int32),
            pltpu.SMEM((ROUTES, TOKENS // STRETCH), jnp.int32),
            dma((2,)),
            pltpu.VMEM((TOKENS // STRETCH, STRETCH, 2 * D), jnp.bfloat16),
            pltpu.VMEM((HALF // STRETCH, STRETCH, D), jnp.bfloat16),
            pltpu.VMEM((4, ROWS, D), jnp.bfloat16),
            pltpu.VMEM((24, ROWS, D), jnp.bfloat16),
            pltpu.VMEM((24, D, 384), jnp.bfloat16),
            pltpu.VMEM((ROWS, 384), jnp.float32),
            pltpu.VMEM((HALF, D), jnp.float32),
            pltpu.VMEM((HALF, D), jnp.float32),
            pltpu.VMEM((HALF, D), jnp.float32),
            dma((3, 3)), dma((4, 3)),
            dma((2, 4, 4)), dma((2, 4, 4)),
            dma((8,)), dma((8,)),
            dma((8, 2)), dma((8,)), dma((2, 2)),
            dma((8,)), dma((8,)),
            dma((4,)), dma((3,)),
            dma((2, 3)), dma((2, 3)),
            dma((2, 3)), dma((2, 3)),
            dma((5, 3)), dma((5, 3)),
        ],
        compiler_params=pltpu.CompilerParams(
            collective_id=0, has_side_effects=True, vmem_limit_bytes=60 * 1024 * 1024),
        cost_estimate=pl.CostEstimate(
            flops=2_400_000_000, bytes_accessed=4_000_000, transcendentals=3_000_000),
    )(*(a.reshape(PER, STRETCH, 384) for a in (query, keys, values)), shot_ids.reshape(TOKENS // SUB, SUB), routes.T, out_weight.reshape(3, D, 3072))


def solution(mesh):
    placed = (P("seq", "head"), P("seq", "head"), P("seq", "head"), P(), P(), P("head", None))
    return jax.shard_map(
        shards, mesh=mesh, in_specs=placed, out_specs=P("seq", "head"), check_vma=False
    )
```

time: 98.5 us -> 84.4 us (0.86)
  the two profiles are of different devices: /device:TPU:57 before, /device:TPU:43 now
where the time goes in v2:
time: 84.4 us; the launch traced here: 84.3 us
  Pallas kernels  82.7 us (98%)
  local copies, waits for them, and re-layouts  1.62 us (2%)
    pallas_call x1, Pallas kernels, shards(): pl.pallas_call(kernel, out_shape=jax.ShapeDtypeStruct((ROWS, 384), jnp.bf...  82.7 us

profile of v2, /device:TPU:43, one launch (start us, length us, event | category | flops | bytes accessed | tf_op | source)
XLA Modules:
  0.0 84.3 jit_solution(17006846652861843363)
XLA Ops:
  0.0 82.7 %shard_map.64 = bf16[256,384]{1,0:T(8,128)(2,1)} custom-call(bf16[4,64,384]{2,1,0:T(8,128)(2,1)} %bitcast.7, bf16[4,64,384]{2,1,0:T(8,128)(2,1)} %bitcast.8, bf16[4,64,384]{2,1,0:T(8,128)(2,1)} %bitcast.9, s32[128,128]{1,0:T(8,128)} %bitcast.10, s32[8,256]{1,0:T(8,128)} %bitcast.11, bf16[3,128,3072]{2,1,0:T(8,128)(2,1)} %bitcast.6), custom_call_target="tpu_custom_call" | custom-call | flops 2400000000 | bytes 4000000 | tf_op jit(solution)/shard_map/pallas_call | solution.py:461
  82.7 1.6 %copy.8 = bf16[256,384]{1,0:T(8,128)(2,1)} copy(bf16[256,384]{1,0:T(8,128)(2,1)} %shard_map.64) | data formatting | bytes 393216

commit v3 on v2

--- a/solution.py
+++ b/solution.py
@@ -117,14 +117,14 @@
     def nth(k, core_of):
         return (y + 2 * ((y // 4 + core_of) % 2) + (0, 1, 3, 2)[k]) % 4
 
-    def piece_of(row, core_of, n):
-        return kv.at[pl.ds((row * NY + 4 * core_of + n) * PER, PER)]
+    def piece_of(row, core_of, n, cut=(0, PER)):
+        return kv.at[pl.ds((row * NY + 4 * core_of + n) * PER + cut[0], cut[1])]
 
     def half_of(row, core_of):
         return kv.at[pl.ds((row * NY + 4 * core_of) * PER, 4 * PER)]
 
-    def to_sibling(o, row, n):
-        ref = piece_of(row, c, n)
+    def to_sibling(o, row, n, cut=(0, PER)):
+        ref = piece_of(row, c, n, cut)
         return remote(ref, ref, sib_s.at[o], sib_r.at[o], sibling)
 
     def hop(way, step, ref, n):
@@ -132,9 +132,16 @@
                       (zr if way == RIGHT else zl, hd))
 
     lean = jnp.logical_xor(core == c, y % 4 == 0)
-
-    def in_ring(n):
-        return jnp.logical_not(jnp.logical_and(lean, n == SPARE))
+    whole, lower, upper = (0, PER), (0, PER // 2), (PER // 2, PER // 2)
+
+    def ring_part(n, fn):
+        @pl.when(n != SPARE)
+        def _():
+            fn(whole)
+
+        @pl.when(jnp.logical_and(n == SPARE, jnp.logical_not(lean)))
+        def _():
+            fn(lower)
 
     def origin(way, step):
         return (z + 8 - 1 - step) % 8 if way == RIGHT else (z + 1 + step) % 8
@@ -207,38 +214,46 @@
     def _():
         def own(k):
             n = nth(k, c)
-            ref = piece_of(z, c, n)
             for t in range(2):
                 arrived(qbuf.at[pl.ds(0, PER)], qr.at[n, t])
 
-            @pl.when(in_ring(n))
-            def _():
+            def begin(cut):
+                ref = piece_of(z, c, n, cut)
                 hop(RIGHT, 0, ref, n).start()
                 hop(LEFT, 0, ref, n).start()
 
+            ring_part(n, begin)
             to_sibling(0, z, n).start()
 
         def pass_on(step, k):
             n = nth(k, c)
 
-            @pl.when(in_ring(n))
-            def _():
+            def carry(cut):
                 for way in (RIGHT, LEFT):
                     if goes(k, way, step):
                         row = origin(way, step)
-                        ref = piece_of(row, c, n)
+                        ref = piece_of(row, c, n, cut)
                         arrived(ref, ring_r.at[way, step, n])
                         if step < 3 and goes(k, way, step + 1):
                             hop(way, step + 1, ref, n).start()
-                        to_sibling(slot(way, step), row, n).start()
+                        to_sibling(slot(way, step), row, n, cut).start()
+
+            ring_part(n, carry)
 
         def handed(step):
-            @pl.when(lean)
-            def _():
+            def take(cut):
                 for way in (RIGHT, LEFT)[:2 if step < 3 else 1]:
                     row = origin(way, step)
-                    arrived(piece_of(row, c, SPARE), hand_r.at[slot(way, step)])
-                    to_sibling(slot(way, step), row, SPARE).start()
+                    arrived(piece_of(row, c, SPARE, cut), hand_r.at[slot(way, step)])
+                    to_sibling(slot(way, step), row, SPARE, cut).start()
+
+            @pl.when(lean)
+            def _():
+                take(whole)
+
+            @pl.when(jnp.logical_not(lean))
+            def _():
+                take(upper)
 
         def from_sibling(o, row):
             arrived(half_of(row, 1 - c), sib_r.at[o])
@@ -249,9 +264,11 @@
         own(2)
         pass_on(0, 1)
         own(3)
-        queries_to_columns()
         pass_on(0, 2)
         pass_on(0, 3)
+        queries_to_columns()
+        for k in range(4):
+            pass_on(1, k)
         handed(0)
         for n in range(4):
             arrived(qbuf.at[pl.ds(0, PER)], qr.at[n, 2])
@@ -259,13 +276,13 @@
         from_sibling(slot(RIGHT, 0), origin(RIGHT, 0))
         from_sibling(slot(LEFT, 0), origin(LEFT, 0))
         for k in range(4):
+            pass_on(2, k)
             pl.loop(2 * k, 2 * k + 2)(shot)
-            pass_on(1, k)
         handed(1)
-        for step in (2, 3):
-            for k in range(4):
-                pass_on(step, k)
-            handed(step)
+        handed(2)
+        for k in range(4):
+            pass_on(3, k)
+        handed(3)
         for step in (1, 2):
             for way in (RIGHT, LEFT):
                 from_sibling(slot(way, step), origin(way, step))
@@ -284,58 +301,58 @@
             def _():
                 pltpu.make_async_copy(att.at[b], piece, back_r.at[y % 4]).start()
 
-    paired = jnp.where(core == c, 1, 0)
-
-    def served(j):
-        return paired * (2 - j), (y + 9 - paired * (2 + j)) % NY
-
     def each(fn):
-        fn(0)
-
-        @pl.when(paired == 1)
-        def _():
-            fn(1)
-
-    def spare_piece(row, j):
-        return kv.at[pl.ds((row * NY + j) * PER, PER)]
-
-    def spare_goes(j, way, step):
-        return step < 3 or j == way
-
-    def hand(o, row, j):
-        return remote(spare_piece(row, j), kv.at[pl.ds((row * NY + y) * PER, PER)],
-                      hand_s.at[o, j], hand_r.at[o],
-                      (z * NY + served(j)[1], 2 * x + core))
+        for i in range(3):
+            near = jnp.logical_xor(core == c, i == 0)
+
+            @pl.when(near)
+            def _():
+                fn(i, whole)
+
+            @pl.when(jnp.logical_not(near))
+            def _():
+                fn(i, upper)
+
+    def spare_piece(row, i, cut):
+        return kv.at[pl.ds((row * NY + i) * PER + cut[0], cut[1])]
+
+    def spare_goes(i, way, step):
+        return step < 3 or i % 2 == way
+
+    def hand(o, row, i, cut):
+        return remote(spare_piece(row, i, cut), kv.at[pl.ds((row * NY + y) * PER + cut[0], cut[1])],
+                      hand_s.at[o, i], hand_r.at[o], (z * NY + 4 * c + i, 2 * x + core))
 
     @pl.when(y % 4 == SPARE)
     def _():
-        def fetch(j):
-            lanes = pl.ds(pl.multiple_of(served(j)[0] * D, D), D)
-            at = pl.ds((z * NY + j) * PER, PER)
-            return [pltpu.make_async_copy(src.at[:, :, lanes], kv.at[at, :, t * D:(t + 1) * D],
-                                          spare_s.at[j, t]) for t, src in enumerate((k_ref, v_ref))]
-
-        def begin(j):
-            for copy in fetch(j):
+        def fetch(i, cut):
+            at = spare_piece(z, i, cut)
+            return [pltpu.make_async_copy(src.at[cut[0]:cut[0] + cut[1], :, i * D:(i + 1) * D],
+                                          at.at[:, :, t * D:(t + 1) * D],
+                                          spare_s.at[i, t]) for t, src in enumerate((k_ref, v_ref))]
+
+        def begin(i, cut):
+            for copy in fetch(i, cut):
                 copy.start()
 
-        def launch(j):
-            for copy in fetch(j):
+        def launch(i, cut):
+            for copy in fetch(i, cut):
                 copy.wait()
             for way in (RIGHT, LEFT):
-                hop(way, 0, spare_piece(z, j), j).start()
+                hop(way, 0, spare_piece(z, i, cut), i).start()
 
         each(begin)
         each(launch)
         for step in range(4):
-            def carry(j):
+            def carry(i, cut):
                 for way in (RIGHT, LEFT):
-                    if spare_goes(j, way, step):
+                    if spare_goes(i, way, step):
                         row = origin(way, step)
-                        arrived(spare_piece(row, j), ring_r.at[way, step, j])
-                        if step < 3 and spare_goes(j, way, step + 1):
-                            hop(way, step + 1, spare_piece(row, j), j).start()
-                        hand(slot(way, step), row, j).start()
+                        ref = spare_piece(row, i, cut)
+                        arrived(ref, ring_r.at[way, step, i])
+                        if step < 3 and spare_goes(i, way, step + 1):
+                            hop(way, step + 1, ref, i).start()
+                        hand(slot(way, step), row, i, cut).start()
 
             each(carry)
             if step == 0:
@@ -425,15 +442,14 @@
             left_for_column(n, 1)
         for k in range(4):
             n = nth(k, c)
-            ref = piece_of(z, c, n)
-
-            @pl.when(in_ring(n))
-            def _():
+
+            def gone(cut):
                 for step in range(4):
                     for way in (RIGHT, LEFT):
                         if goes(k, way, step):
-                            hop(way, step, ref, n).wait_send()
-
+                            hop(way, step, piece_of(z, c, n, cut), n).wait_send()
+
+            ring_part(n, gone)
         for o in range(8):
             sent(half_of(z, c), sib_s.at[o])
         for k in range(4):
@@ -445,12 +461,12 @@
 
     @pl.when(y % 4 == SPARE)
     def _():
-        def gone(j):
+        def gone(i, cut):
             for step in range(4):
                 for way in (RIGHT, LEFT):
-                    if spare_goes(j, way, step):
-                        hop(way, step, spare_piece(z, j), j).wait_send()
-                        hand(slot(way, step), z, j).wait_send()
+                    if spare_goes(i, way, step):
+                        hop(way, step, spare_piece(z, i, cut), i).wait_send()
+                        hand(slot(way, step), z, i, cut).wait_send()
 
         each(gone)
 
@@ -479,7 +495,7 @@
             dma((3, 3)), dma((4, 3)),
             dma((2, 4, 4)), dma((2, 4, 4)),
             dma((8,)), dma((8,)),
-            dma((8, 2)), dma((8,)), dma((2, 2)),
+            dma((8, 3)), dma((8,)), dma((3, 2)),
             dma((8,)), dma((8,)),
             dma((4,)), dma((3,)),
             dma((2, 3)), dma((2, 3)),

time: 84.4 us -> 81.8 us (0.969)
  the two profiles are of different devices: /device:TPU:43 before, /device:TPU:35 now
where the time goes in v3:
time: 81.8 us; the launch traced here: 81.6 us
  Pallas kernels  80 us (98%)
  local copies, waits for them, and re-layouts  1.62 us (2%)
    pallas_call x1, Pallas kernels, shards(): pl.pallas_call(kernel, out_shape=jax.ShapeDtypeStruct((ROWS, 384), jnp.bf...  80 us

profile of v3, /device:TPU:35, one launch (start us, length us, event | category | flops | bytes accessed | tf_op | source)
XLA Modules:
  0.0 81.6 jit_solution(18066411334226545787)
XLA Ops:
  0.0 80.0 %shard_map.64 = bf16[256,384]{1,0:T(8,128)(2,1)} custom-call(bf16[4,64,384]{2,1,0:T(8,128)(2,1)} %bitcast.7, bf16[4,64,384]{2,1,0:T(8,128)(2,1)} %bitcast.8, bf16[4,64,384]{2,1,0:T(8,128)(2,1)} %bitcast.9, s32[128,128]{1,0:T(8,128)} %bitcast.10, s32[8,256]{1,0:T(8,128)} %bitcast.11, bf16[3,128,3072]{2,1,0:T(8,128)(2,1)} %bitcast.6), custom_call_target="tpu_custom_call" | custom-call | flops 2400000000 | bytes 4000000 | tf_op jit(solution)/shard_map/pallas_call | solution.py:477
  80.0 1.6 %copy.8 = bf16[256,384]{1,0:T(8,128)(2,1)} copy(bf16[256,384]{1,0:T(8,128)(2,1)} %shard_map.64) | data formatting | bytes 393216

commit v4 on v3

--- a/solution.py
+++ b/solution.py
@@ -264,9 +264,9 @@
         own(2)
         pass_on(0, 1)
         own(3)
+        queries_to_columns()
         pass_on(0, 2)
         pass_on(0, 3)
-        queries_to_columns()
         for k in range(4):
             pass_on(1, k)
         handed(0)
@@ -414,10 +414,12 @@
     w_own.wait()
     for d in range(1, 8):
         arrived(w_here, w_r.at[d])
-    for turn in range(7):
-        for late, stage in enumerate((from_columns, from_beside, from_far, project_own)):
+    for turn in range(6):
+        for late, stage in enumerate((from_columns, from_beside, from_far)):
             if 0 <= turn - late < 4:
                 in_turn(turn - late, stage)
+    for turn in range(4):
+        in_turn(turn, project_own)
     for turn in range(4):
         in_turn(turn, project_sibling)
 

time: 81.8 us -> 82.3 us (level)
  no operation moved by 1% of the time
where the time goes in v4:
time: 82.3 us; the launch traced here: 82.1 us
  Pallas kernels  80.5 us (98%)
  local copies, waits for them, and re-layouts  1.62 us (2%)
    pallas_call x1, Pallas kernels, shards(): pl.pallas_call(kernel, out_shape=jax.ShapeDtypeStruct((ROWS, 384), jnp.bf...  80.5 us

profile of v4, /device:TPU:35, one launch (start us, length us, event | category | flops | bytes accessed | tf_op | source)
XLA Modules:
  0.0 82.1 jit_solution(12036329554289497318)
XLA Ops:
  0.0 80.5 %shard_map.64 = bf16[256,384]{1,0:T(8,128)(2,1)} custom-call(bf16[4,64,384]{2,1,0:T(8,128)(2,1)} %bitcast.7, bf16[4,64,384]{2,1,0:T(8,128)(2,1)} %bitcast.8, bf16[4,64,384]{2,1,0:T(8,128)(2,1)} %bitcast.9, s32[128,128]{1,0:T(8,128)} %bitcast.10, s32[8,256]{1,0:T(8,128)} %bitcast.11, bf16[3,128,3072]{2,1,0:T(8,128)(2,1)} %bitcast.6), custom_call_target="tpu_custom_call" | custom-call | flops 2400000000 | bytes 4000000 | tf_op jit(solution)/shard_map/pallas_call | solution.py:479
  80.5 1.6 %copy.8 = bf16[256,384]{1,0:T(8,128)(2,1)} copy(bf16[256,384]{1,0:T(8,128)(2,1)} %shard_map.64) | data formatting | bytes 393216

commit v5 on v3

--- a/solution.py
+++ b/solution.py
@@ -52,6 +52,17 @@
     ids_copy.start()
     routes_copy.start()
 
+    @pl.when(y == 4 * c + y % 4)
+    def _():
+        @pl.when(y % 4 < SPARE)
+        def _():
+            lanes = pl.ds(pl.multiple_of(y % 4 * D, D), D)
+            for t, (src, dst) in enumerate((
+                    (k_ref, kv.at[pl.ds(p * PER, PER), :, 0:D]),
+                    (v_ref, kv.at[pl.ds(p * PER, PER), :, D:2 * D]),
+                    (q_ref, qbuf.at[pl.ds(y % 4 * PER, PER)]))):
+                pltpu.make_async_copy(src.at[:, :, lanes], dst, qr.at[y % 4, t]).start()
+
     barrier = pltpu.get_barrier_semaphore()
     peers = [sibling]
     for d in range(1, NY):
@@ -83,10 +94,6 @@
         @pl.when(jnp.logical_not(own))
         def _():
             remote(part, dst, qs.at[n, t], qr.at[y % 4, t], (z * NY + h, 2 * x + core)).start()
-
-        @pl.when(own)
-        def _():
-            pltpu.make_async_copy(part, dst, qr.at[y % 4, t]).start()
 
     def left_for_column(n, t):
         h = 4 * c + n + turned * (2 - 2 * n)

time: 81.8 us -> 81.8 us (level)
  no operation moved by 1% of the time
where the time goes in v5:
time: 81.8 us; the launch traced here: 81.7 us
  Pallas kernels  80.1 us (98%)
  local copies, waits for them, and re-layouts  1.62 us (2%)
    pallas_call x1, Pallas kernels, shards(): pl.pallas_call(kernel, out_shape=jax.ShapeDtypeStruct((ROWS, 384), jnp.bf...  80.1 us

profile of v5, /device:TPU:35, one launch (start us, length us, event | category | flops | bytes accessed | tf_op | source)
XLA Modules:
  0.0 81.7 jit_solution(18020182492780181968)
XLA Ops:
  0.0 80.1 %shard_map.64 = bf16[256,384]{1,0:T(8,128)(2,1)} custom-call(bf16[4,64,384]{2,1,0:T(8,128)(2,1)} %bitcast.7, bf16[4,64,384]{2,1,0:T(8,128)(2,1)} %bitcast.8, bf16[4,64,384]{2,1,0:T(8,128)(2,1)} %bitcast.9, s32[128,128]{1,0:T(8,128)} %bitcast.10, s32[8,256]{1,0:T(8,128)} %bitcast.11, bf16[3,128,3072]{2,1,0:T(8,128)(2,1)} %bitcast.6), custom_call_target="tpu_custom_call" | custom-call | flops 2400000000 | bytes 4000000 | tf_op jit(solution)/shard_map/pallas_call | solution.py:484
  80.1 1.6 %copy.8 = bf16[256,384]{1,0:T(8,128)(2,1)} copy(bf16[256,384]{1,0:T(8,128)(2,1)} %shard_map.64) | data formatting | bytes 393216
